TPU v7x, 32 devices: a whole 2x2x4 slice. The times are simulated.
32 devices in a mesh: req: 16 (over z, y, core), tp: 2 (over x).
Axes of the slice: x: 2, y: 2, z: 4, core: 2. Of those that a mesh axis runs over, the one named last changes fastest.
Arguments:
- hidden_in: bfloat16 [32768, 1536], P(('req', 'tp')), may hold values from -30 to 30
- segment_ids: int32 [32768], P('req'), may hold values from 0 to 9, as said below
- page_owner: int32 [512], P('req'), may hold values from 0 to 15, as said below
- norm_gain: bfloat16 [1536], replicated, may hold values from 0.099609375 to 1.8984375
- w_qkv: bfloat16 [1536, 1536], P(None, 'tp'), may hold values from -16 to 16
- w_out: bfloat16 [768, 1536], P('tp'), may hold values from -0.625 to 0.625
Outputs:
- hidden_out: bfloat16 [32768, 1536], P(('req', 'tp'))
- kv_cache: bfloat16 [512, 4, 2, 6144], P('req', 'tp')
Inputs may be any that keep to these rules, and one draw needn't show every extreme that they name: `segment_ids`: within a group the numbers never fall. 0 marks the shared prefix, which comes first with 128 to 512 tokens; 1 to 8 mark the requests (a request may be empty); 9 marks padding at the end. At least three quarters of each group's tokens are not padding, and some group has none. `page_owner`: for each page number p, the 16 groups name 16 different owners for their page p. A group names one owner for at most 2 of its pages.
All inputs are finite; a program needn't handle non-finite values.
Results may differ from a plain program's by a relative error of at most 0.0095.
Values may be sent and summed in bfloat16 or wider, within the bound.
A program may use at most 128 MiB of HBM per device.

v0:
```python
import math

import jax
import jax.numpy as jnp
from jax import lax
from jax.sharding import PartitionSpec as P

HEAD = 96
HEADS_Q = 8
HEADS_KV = 4
PAGE = 64
REQS = 8


rotary_base = 100000.0
norm_eps = 1e-05
masked_score = -1e30


def positions_of(segments):
    length = segments.shape[0]
    counter = jnp.arange(length, dtype=jnp.int32)
    previous = jnp.concatenate([segments[:1] - 1, segments[:-1]])
    starts = lax.cummax(jnp.where(segments != previous, counter, 0), axis=0)
    prefix_len = jnp.sum((segments == 0).astype(jnp.int32))
    return counter - starts + jnp.where(segments > 0, prefix_len, 0)


def rotary_tables(positions, width):
    half_width = width // 2
    exponent = jnp.arange(half_width, dtype=jnp.float32) * (2.0 / width)
    inverse = jnp.power(jnp.float32(rotary_base), -exponent)
    angles = positions.astype(jnp.float32)[:, None] * inverse[None, :]
    return (jnp.cos(angles), jnp.sin(angles))


def rotate(vectors, cosine, sine_table):
    half_width = vectors.shape[-1] // 2
    front_half = vectors[..., :half_width]
    second = vectors[..., half_width:]
    cosine = cosine[:, None, :]
    sine_table = sine_table[:, None, :]
    return jnp.concatenate(
        [front_half * cosine - second * sine_table, second * cosine + front_half * sine_table],
        axis=-1,
    )


def normalize(token_rows, gain_vector):
    values = token_rows.astype(jnp.float32)
    inverse_root = lax.rsqrt(jnp.mean(values * values, axis=-1, keepdims=True) + norm_eps)
    return (values * inverse_root * gain_vector.astype(jnp.float32)).astype(jnp.bfloat16)


def attend(queries, key_vectors, value_vectors, query_segments, key_segments, query_offset):
    query_count = queries.shape[0]
    query_heads = queries.shape[1]
    head_width = queries.shape[2]
    key_count = key_vectors.shape[0]
    key_heads = key_vectors.shape[1]
    group_ratio = query_heads // key_heads
    query_block = math.gcd(query_count, max(8, 1024 // query_heads))
    factor = head_width ** (-0.5)
    grouped = queries.reshape(
        query_count // query_block, query_block, key_heads, group_ratio, head_width
    )
    segment_blocks = query_segments.reshape(query_count // query_block, query_block)
    key_places = jnp.arange(key_count, dtype=jnp.int32)

    def one_block(inputs):
        block_queries, block_segments, block_number = inputs
        query_start = query_offset + block_number * query_block
        query_places = query_start + jnp.arange(query_block, dtype=jnp.int32)
        allowed = (key_places[None, :] <= query_places[:, None]) & (
            (key_segments[None, :] == block_segments[:, None]) | (key_segments[None, :] == 0)
        )
        raw_scores = (
            jnp.einsum(
                "qhgd,khd->hgqk", block_queries, key_vectors, preferred_element_type=jnp.float32
            )
            * factor
        )
        masked = jnp.where(allowed, raw_scores, masked_score)
        row_max = jnp.max(masked, axis=-1, keepdims=True)
        weights = jnp.where(allowed, jnp.exp(masked - row_max), 0.0)
        totals = jnp.sum(weights, axis=-1)
        mixed_sum = jnp.einsum(
            "hgqk,khd->qhgd",
            weights.astype(jnp.bfloat16),
            value_vectors,
            preferred_element_type=jnp.float32,
        )
        result = mixed_sum / jnp.transpose(totals, (2, 0, 1))[..., None]
        return result.astype(jnp.bfloat16).reshape(query_block, query_heads * head_width)

    numbers = jnp.arange(query_count // query_block, dtype=jnp.int32)
    outputs = lax.map(one_block, (grouped, segment_blocks, numbers))
    return outputs.reshape(query_count, query_heads * head_width)


def shards(hidden_in, segment_ids, page_owner, norm_gain, w_qkv, w_out):
    tp_count = lax.axis_size("tp")
    req_count = lax.axis_size("req")
    group_len = segment_ids.shape[0]
    local_query = HEADS_Q // tp_count
    local_kv = HEADS_KV // tp_count
    query_width = local_query * HEAD
    kv_width = local_kv * HEAD
    positions = positions_of(segment_ids)
    cosine, sine_table = rotary_tables(positions, HEAD)
    normed_own = normalize(hidden_in, norm_gain)
    normed_all = lax.all_gather(normed_own, "tp", axis=0, tiled=True)
    projected = jnp.dot(normed_all, w_qkv, preferred_element_type=jnp.float32)
    queries = rotate(
        projected[:, :query_width].reshape(group_len, local_query, HEAD), cosine, sine_table
    ).astype(jnp.bfloat16)
    keys_local = rotate(
        projected[:, query_width : query_width + kv_width].reshape(group_len, local_kv, HEAD),
        cosine,
        sine_table,
    ).astype(jnp.bfloat16)
    values_local = (
        projected[:, query_width + kv_width :]
        .reshape(group_len, local_kv, HEAD)
        .astype(jnp.bfloat16)
    )
    attended = attend(queries, keys_local, values_local, segment_ids, segment_ids, 0)
    projected_out = lax.psum_scatter(
        jnp.dot(attended, w_out, preferred_element_type=jnp.float32).astype(jnp.bfloat16),
        "tp",
        scatter_dimension=0,
        tiled=True,
    ).astype(jnp.float32)
    hidden_out = (hidden_in.astype(jnp.float32) + projected_out).astype(jnp.bfloat16)
    page_count = group_len // PAGE
    lane_count = -(-page_count // req_count)
    key_pages = (
        keys_local.reshape(page_count, PAGE, local_kv, HEAD)
        .transpose(0, 2, 1, 3)
        .reshape(page_count, local_kv, PAGE * HEAD)
    )
    value_pages = (
        values_local.reshape(page_count, PAGE, local_kv, HEAD)
        .transpose(0, 2, 1, 3)
        .reshape(page_count, local_kv, PAGE * HEAD)
    )
    page_data = jnp.stack([key_pages, value_pages], axis=2).reshape(
        page_count, local_kv * 2 * PAGE * HEAD
    )
    live_pages = segment_ids[::PAGE] != REQS + 1
    page_numbers = jnp.arange(page_count, dtype=jnp.int32)
    same_owner = (
        (page_owner[:, None] == page_owner[None, :])
        & live_pages[None, :]
        & (page_numbers[None, :] < page_numbers[:, None])
    )
    page_rank = jnp.sum(same_owner.astype(jnp.int32), axis=1)
    owner_ids = jnp.arange(req_count, dtype=jnp.int32)
    lane_ids = jnp.arange(lane_count, dtype=jnp.int32)
    selection = (
        (page_owner[None, None, :] == owner_ids[:, None, None])
        & (page_rank[None, None, :] == lane_ids[None, :, None])
        & live_pages[None, None, :]
    )
    send_pages = jnp.einsum(
        "olp,pc->olc", selection.astype(jnp.bfloat16), page_data, preferred_element_type=jnp.float32
    ).astype(jnp.bfloat16)
    send_ids = jnp.sum(jnp.where(selection, page_numbers[None, None, :] + 1, 0), axis=2) - 1
    received, received_ids = (
        lax.all_to_all(send_pages, "req", split_axis=0, concat_axis=0, tiled=True),
        lax.all_to_all(send_ids, "req", split_axis=0, concat_axis=0, tiled=True),
    )
    placing = (
        received_ids.reshape(req_count * lane_count)[None, :] == page_numbers[:, None]
    ).astype(jnp.bfloat16)
    cache_rows = jnp.dot(
        placing,
        received.reshape(req_count * lane_count, local_kv * 2 * PAGE * HEAD),
        preferred_element_type=jnp.float32,
    ).astype(jnp.bfloat16)
    return (hidden_out, cache_rows.reshape(page_count, local_kv, 2, PAGE * HEAD))


def solution(mesh):
    placed = (P(("req", "tp"), None), P("req"), P("req"), P(), P(None, "tp"), P("tp", None))
    return jax.shard_map(
        shards,
        mesh=mesh,
        in_specs=placed,
        out_specs=(P(("req", "tp"), None), P("req", "tp", None, None)),
        check_vma=False,
    )
```

profile of v0, /device:TPU:14, one launch (start us, length us, event | category | flops | bytes accessed | tf_op | source)
XLA Modules:
  0.0 311.9 jit_solution(17138899405926749725)
XLA Ops:
  7.2 2.7 fusion.47
  10.2 2.4 fusion.49
  17.8 75.6 %all-gather.2.cloned.1.call-done = bf16[2048,1536]{1,0:T(8,128)(2,1)} async-done(((bf16[1024,1536]{1,0:T(8,128)(2,1)}), bf16[2048,1536]{1,0:T(8,128)(2,1)}) %all-gather.2.cloned.1.call-update) | async-done | bytes 6291472 | tf_op jit(solution)/shard_map/all_gather | solution.py:112
  93.4 7.4 %fusion.67 = f32[2048,768]{0,1:T(8,128)S(1)} fusion(bf16[2048,1536]{1,0:T(8,128)(2,1)} %all-gather.2.cloned.1.call-done, bf16[1536,768]{1,0:T(8,128)(2,1)S(1)} %copy-done), kind=kOutput, calls=%fused_computation.81 | convolution fusion | flops 4831838208 | bytes 14942208 | tf_op jit(solution)/shard_map/dot_general | solution.py:113
  100.9 2.5 copy-done.3
  109.1 105.4 %while.11 = (s32[]{:T(128)}, bf16[8,256,384]{2,1,0:T(8,128)(2,1)}, s32[8]{0:T(128)S(1)}, s32[2048]{0:T(1024)S(1)}, s32[8,256]{1,0:T(8,128)S(1)}, /*index=5*/bf16...) while((s32[]{:T(128)}, bf16[8,256,384]{2,1,0:T(8,128)(2,1)}, ...), condition=%wide.region_7.8_spmd.clone, body=%wide.region_4.7_spmd.clone.sunk | while | flops 820187392 | bytes 12748933 | solution.py:97
  111.1 6.7 %fusion.87 = (f32[2,2,256]{2,1,0:T(2,128)S(1)}, bf16[2,2,256,2048]{3,2,1,0:T(8,128)(2,1)}) fusion(pred[256,2048]{1,0:T(8,128)(4,1)S(1)} %fusion.86, bf16[2048,2,96]{0,2,1:T(8,128)(2,1)S(1)} %get-tuple-element.199, bf16[8,256,2,2,96]{1,4,3,2,0:T(8,128)(2,1)} %get-tuple-element.198, s32[]{:T(128)} %get-tuple-element.183), kind=kOutput, calls=%fused_computation.80.clone.1 | convolution fusion | flops 415238144 | bytes 6230528 | tf_op jit(solution)/shard_map/while/body/eval_jaxpr/sub | solution.py:85
  117.8 3.6 %fusion.88 = bf16[256,2,2,96]{0,3,2,1:T(8,128)(2,1)S(1)} fusion(bf16[2,2,256,2048]{3,2,1,0:T(8,128)(2,1)} %get-tuple-element.171, bf16[2048,2,96]{0,2,1:T(8,128)(2,1)S(1)} %get-tuple-element.200, f32[256,2,2]{0,2,1:T(2,128)S(1)} %bitcast.135), kind=kOutput, calls=%fused_computation.18.clone.1 | convolution fusion | flops 402849792 | bytes 5181440 | tf_op jit(solution)/shard_map/while/body/eval_jaxpr/hgqk,khd->qhgd/dot_general | solution.py:87
  124.3 6.7 %fusion.87 = (f32[2,2,256]{2,1,0:T(2,128)S(1)}, bf16[2,2,256,2048]{3,2,1,0:T(8,128)(2,1)}) fusion(pred[256,2048]{1,0:T(8,128)(4,1)S(1)} %fusion.86, bf16[2048,2,96]{0,2,1:T(8,128)(2,1)S(1)} %get-tuple-element.199, bf16[8,256,2,2,96]{1,4,3,2,0:T(8,128)(2,1)} %get-tuple-element.198, s32[]{:T(128)} %get-tuple-element.183), kind=kOutput, calls=%fused_computation.80.clone.1 | convolution fusion | flops 415238144 | bytes 6230528 | tf_op jit(solution)/shard_map/while/body/eval_jaxpr/sub | solution.py:85
  131.0 3.6 %fusion.88 = bf16[256,2,2,96]{0,3,2,1:T(8,128)(2,1)S(1)} fusion(bf16[2,2,256,2048]{3,2,1,0:T(8,128)(2,1)} %get-tuple-element.171, bf16[2048,2,96]{0,2,1:T(8,128)(2,1)S(1)} %get-tuple-element.200, f32[256,2,2]{0,2,1:T(2,128)S(1)} %bitcast.135), kind=kOutput, calls=%fused_computation.18.clone.1 | convolution fusion | flops 402849792 | bytes 5181440 | tf_op jit(solution)/shard_map/while/body/eval_jaxpr/hgqk,khd->qhgd/dot_general | solution.py:87
  137.5 6.7 %fusion.87 = (f32[2,2,256]{2,1,0:T(2,128)S(1)}, bf16[2,2,256,2048]{3,2,1,0:T(8,128)(2,1)}) fusion(pred[256,2048]{1,0:T(8,128)(4,1)S(1)} %fusion.86, bf16[2048,2,96]{0,2,1:T(8,128)(2,1)S(1)} %get-tuple-element.199, bf16[8,256,2,2,96]{1,4,3,2,0:T(8,128)(2,1)} %get-tuple-element.198, s32[]{:T(128)} %get-tuple-element.183), kind=kOutput, calls=%fused_computation.80.clone.1 | convolution fusion | flops 415238144 | bytes 6230528 | tf_op jit(solution)/shard_map/while/body/eval_jaxpr/sub | solution.py:85
  144.1 3.6 %fusion.88 = bf16[256,2,2,96]{0,3,2,1:T(8,128)(2,1)S(1)} fusion(bf16[2,2,256,2048]{3,2,1,0:T(8,128)(2,1)} %get-tuple-element.171, bf16[2048,2,96]{0,2,1:T(8,128)(2,1)S(1)} %get-tuple-element.200, f32[256,2,2]{0,2,1:T(2,128)S(1)} %bitcast.135), kind=kOutput, calls=%fused_computation.18.clone.1 | convolution fusion | flops 402849792 | bytes 5181440 | tf_op jit(solution)/shard_map/while/body/eval_jaxpr/hgqk,khd->qhgd/dot_general | solution.py:87
  150.6 6.7 %fusion.87 = (f32[2,2,256]{2,1,0:T(2,128)S(1)}, bf16[2,2,256,2048]{3,2,1,0:T(8,128)(2,1)}) fusion(pred[256,2048]{1,0:T(8,128)(4,1)S(1)} %fusion.86, bf16[2048,2,96]{0,2,1:T(8,128)(2,1)S(1)} %get-tuple-element.199, bf16[8,256,2,2,96]{1,4,3,2,0:T(8,128)(2,1)} %get-tuple-element.198, s32[]{:T(128)} %get-tuple-element.183), kind=kOutput, calls=%fused_computation.80.clone.1 | convolution fusion | flops 415238144 | bytes 6230528 | tf_op jit(solution)/shard_map/while/body/eval_jaxpr/sub | solution.py:85
  157.3 3.6 %fusion.88 = bf16[256,2,2,96]{0,3,2,1:T(8,128)(2,1)S(1)} fusion(bf16[2,2,256,2048]{3,2,1,0:T(8,128)(2,1)} %get-tuple-element.171, bf16[2048,2,96]{0,2,1:T(8,128)(2,1)S(1)} %get-tuple-element.200, f32[256,2,2]{0,2,1:T(2,128)S(1)} %bitcast.135), kind=kOutput, calls=%fused_computation.18.clone.1 | convolution fusion | flops 402849792 | bytes 5181440 | tf_op jit(solution)/shard_map/while/body/eval_jaxpr/hgqk,khd->qhgd/dot_general | solution.py:87
  163.8 6.7 %fusion.87 = (f32[2,2,256]{2,1,0:T(2,128)S(1)}, bf16[2,2,256,2048]{3,2,1,0:T(8,128)(2,1)}) fusion(pred[256,2048]{1,0:T(8,128)(4,1)S(1)} %fusion.86, bf16[2048,2,96]{0,2,1:T(8,128)(2,1)S(1)} %get-tuple-element.199, bf16[8,256,2,2,96]{1,4,3,2,0:T(8,128)(2,1)} %get-tuple-element.198, s32[]{:T(128)} %get-tuple-element.183), kind=kOutput, calls=%fused_computation.80.clone.1 | convolution fusion | flops 415238144 | bytes 6230528 | tf_op jit(solution)/shard_map/while/body/eval_jaxpr/sub | solution.py:85
  170.5 3.6 %fusion.88 = bf16[256,2,2,96]{0,3,2,1:T(8,128)(2,1)S(1)} fusion(bf16[2,2,256,2048]{3,2,1,0:T(8,128)(2,1)} %get-tuple-element.171, bf16[2048,2,96]{0,2,1:T(8,128)(2,1)S(1)} %get-tuple-element.200, f32[256,2,2]{0,2,1:T(2,128)S(1)} %bitcast.135), kind=kOutput, calls=%fused_computation.18.clone.1 | convolution fusion | flops 402849792 | bytes 5181440 | tf_op jit(solution)/shard_map/while/body/eval_jaxpr/hgqk,khd->qhgd/dot_general | solution.py:87
  177.0 6.7 %fusion.87 = (f32[2,2,256]{2,1,0:T(2,128)S(1)}, bf16[2,2,256,2048]{3,2,1,0:T(8,128)(2,1)}) fusion(pred[256,2048]{1,0:T(8,128)(4,1)S(1)} %fusion.86, bf16[2048,2,96]{0,2,1:T(8,128)(2,1)S(1)} %get-tuple-element.199, bf16[8,256,2,2,96]{1,4,3,2,0:T(8,128)(2,1)} %get-tuple-element.198, s32[]{:T(128)} %get-tuple-element.183), kind=kOutput, calls=%fused_computation.80.clone.1 | convolution fusion | flops 415238144 | bytes 6230528 | tf_op jit(solution)/shard_map/while/body/eval_jaxpr/sub | solution.py:85
  183.7 3.6 %fusion.88 = bf16[256,2,2,96]{0,3,2,1:T(8,128)(2,1)S(1)} fusion(bf16[2,2,256,2048]{3,2,1,0:T(8,128)(2,1)} %get-tuple-element.171, bf16[2048,2,96]{0,2,1:T(8,128)(2,1)S(1)} %get-tuple-element.200, f32[256,2,2]{0,2,1:T(2,128)S(1)} %bitcast.135), kind=kOutput, calls=%fused_computation.18.clone.1 | convolution fusion | flops 402849792 | bytes 5181440 | tf_op jit(solution)/shard_map/while/body/eval_jaxpr/hgqk,khd->qhgd/dot_general | solution.py:87
  190.1 6.7 %fusion.87 = (f32[2,2,256]{2,1,0:T(2,128)S(1)}, bf16[2,2,256,2048]{3,2,1,0:T(8,128)(2,1)}) fusion(pred[256,2048]{1,0:T(8,128)(4,1)S(1)} %fusion.86, bf16[2048,2,96]{0,2,1:T(8,128)(2,1)S(1)} %get-tuple-element.199, bf16[8,256,2,2,96]{1,4,3,2,0:T(8,128)(2,1)} %get-tuple-element.198, s32[]{:T(128)} %get-tuple-element.183), kind=kOutput, calls=%fused_computation.80.clone.1 | convolution fusion | flops 415238144 | bytes 6230528 | tf_op jit(solution)/shard_map/while/body/eval_jaxpr/sub | solution.py:85
  196.8 3.6 %fusion.88 = bf16[256,2,2,96]{0,3,2,1:T(8,128)(2,1)S(1)} fusion(bf16[2,2,256,2048]{3,2,1,0:T(8,128)(2,1)} %get-tuple-element.171, bf16[2048,2,96]{0,2,1:T(8,128)(2,1)S(1)} %get-tuple-element.200, f32[256,2,2]{0,2,1:T(2,128)S(1)} %bitcast.135), kind=kOutput, calls=%fused_computation.18.clone.1 | convolution fusion | flops 402849792 | bytes 5181440 | tf_op jit(solution)/shard_map/while/body/eval_jaxpr/hgqk,khd->qhgd/dot_general | solution.py:87
  203.3 6.7 %fusion.87 = (f32[2,2,256]{2,1,0:T(2,128)S(1)}, bf16[2,2,256,2048]{3,2,1,0:T(8,128)(2,1)}) fusion(pred[256,2048]{1,0:T(8,128)(4,1)S(1)} %fusion.86, bf16[2048,2,96]{0,2,1:T(8,128)(2,1)S(1)} %get-tuple-element.199, bf16[8,256,2,2,96]{1,4,3,2,0:T(8,128)(2,1)} %get-tuple-element.198, s32[]{:T(128)} %get-tuple-element.183), kind=kOutput, calls=%fused_computation.80.clone.1 | convolution fusion | flops 415238144 | bytes 6230528 | tf_op jit(solution)/shard_map/while/body/eval_jaxpr/sub | solution.py:85
  210.0 3.6 %fusion.88 = bf16[256,2,2,96]{0,3,2,1:T(8,128)(2,1)S(1)} fusion(bf16[2,2,256,2048]{3,2,1,0:T(8,128)(2,1)} %get-tuple-element.171, bf16[2048,2,96]{0,2,1:T(8,128)(2,1)S(1)} %get-tuple-element.200, f32[256,2,2]{0,2,1:T(2,128)S(1)} %bitcast.135), kind=kOutput, calls=%fused_computation.18.clone.1 | convolution fusion | flops 402849792 | bytes 5181440 | tf_op jit(solution)/shard_map/while/body/eval_jaxpr/hgqk,khd->qhgd/dot_general | solution.py:87
  214.5 7.8 %convolution_convert_fusion.2 = bf16[2048,1536]{1,0:T(8,128)(2,1)} fusion(bf16[2048,384]{1,0:T(8,128)(2,1)} %bitcast.134, bf16[384,1536]{1,0:T(8,128)(2,1)} %param.13), kind=kOutput, calls=%fused_computation.40 | convolution fusion | flops 2419064832 | bytes 9043968 | tf_op jit(solution)/shard_map/dot_general | solution.py:129
  224.0 6.1 %all-to-all-start = ((s32[16,1,2]{2,1,0:T(1,128)}), s32[16,1,2]{2,1,0:T(1,128)S(1)}, u32[]{:S(2)}, u32[]{:S(2)}) async-start(s32[16,1,2]{2,1,0:T(1,128)} %copy.30), calls=%async_computation.1 | async-start | bytes 16384 | tf_op jit(solution)/shard_map/all_to_all | solution.py:171
  233.9 2.3 stack_reshape.6
  238.6 2.8 copy.35
  241.4 2.4 reshape.211
  244.4 2.8 copy.36
  247.2 6.0 %all-to-all-start.1 = ((bf16[16,2,24576]{2,1,0:T(2,128)(2,1)}), bf16[16,2,24576]{2,1,0:T(2,128)(2,1)S(1)}, u32[]{:S(2)}, u32[]{:S(2)}) async-start(bf16[16,2,24576]{2,1,0:T(2,128)(2,1)} %copy.36), calls=%async_computation.2 | async-start | bytes 3145728 | tf_op jit(solution)/shard_map/all_to_all | solution.py:170
  254.5 34.8 %all-to-all-done.1 = bf16[16,2,24576]{2,1,0:T(2,128)(2,1)S(1)} async-done(((bf16[16,2,24576]{2,1,0:T(2,128)(2,1)}), bf16[16,2,24576]{2,1,0:T(2,128)(2,1)S(1)}, u32[]{:S(2)}, u32[]{:S(2)}) %all-to-all-start.1) | async-done | bytes 1572896 | tf_op jit(solution)/shard_map/all_to_all | solution.py:170
  294.8 4.8 %reduce-scatter.2.cloned.1.call-done = bf16[1024,1536]{1,0:T(8,128)(2,1)} async-done(((bf16[2048,1536]{1,0:T(8,128)(2,1)}), bf16[1024,1536]{1,0:T(8,128)(2,1)}) %reduce-scatter.2.cloned.1.call-update) | async-done | bytes 3145744 | tf_op jit(solution)/shard_map/reduce_scatter | solution.py:128
  299.6 5.5 %fusion.50 = bf16[1024,1536]{1,0:T(8,128)(2,1)} fusion(bf16[1024,1536]{1,0:T(8,128)(2,1)} %param.8, bf16[1024,1536]{1,0:T(8,128)(2,1)} %reduce-scatter.2.cloned.1.call-done), kind=kLoop, calls=%fused_computation.44 | loop fusion | flops 6291456 | bytes 9437184 | tf_op jit(solution)/shard_map/convert_element_type | solution.py:134
  (133 shorter events, 43.2 us)
Async XLA Ops:
  7.2 86.2 %copy-start = (bf16[1536,768]{1,0:T(8,128)(2,1)S(1)}, bf16[1536,768]{1,0:T(8,128)(2,1)}, u32[]{:S(2)}) copy-start(bf16[1536,768]{1,0:T(8,128)(2,1)} %param.12) | copy-start | bytes 7077892
  7.2 2.8 copy-start.11
  7.2 86.2 %all-gather.2.cloned.1.call-start = ((), (), s32[]{:S(2)}) async-start(), calls=%async_computation.3 | async-start | bytes 9437184 | tf_op jit(solution)/shard_map/all_gather | solution.py:112
  7.2 2.9 copy-start.2
  12.6 0.7 copy-start.9
  12.7 287.0 %reduce-scatter.2.cloned.1.call-start = ((), (), s32[]{:S(2)}) async-start(), calls=%async_computation.4 | async-start | bytes 9437184 | tf_op jit(solution)/shard_map/reduce_scatter | solution.py:128
  100.8 2.7 copy-start.3
  104.4 2.0 slice-start
  104.6 4.4 %copy-start.5 = (bf16[2048,2,48]{0,2,1:T(8,128)(2,1)}, bf16[2048,2,48]{0,2,1:T(8,128)(2,1)S(1)}, u32[]{:S(2)}) copy-start(bf16[2048,2,48]{0,2,1:T(8,128)(2,1)S(1)} %get-tuple-element.113) | copy-start | bytes 1179652
  107.5 1.6 copy-start.7
  222.3 0.7 copy-start.10
  222.3 8.2 %copy-start.6 = (bf16[2048,2,48]{0,2,1:T(8,128)(2,1)S(1)}, bf16[2048,2,48]{0,2,1:T(8,128)(2,1)}, u32[]{:S(2)}) copy-start(bf16[2048,2,48]{0,2,1:T(8,128)(2,1)} %copy-done.5) | copy-start | bytes 1179652
  224.0 23.2 %all-to-all-start = ((s32[16,1,2]{2,1,0:T(1,128)}), s32[16,1,2]{2,1,0:T(1,128)S(1)}, u32[]{:S(2)}, u32[]{:S(2)}) async-start(s32[16,1,2]{2,1,0:T(1,128)} %copy.30), calls=%async_computation.1 | async-start | bytes 16384 | tf_op jit(solution)/shard_map/all_to_all | solution.py:171
  233.8 2.3 copy-start.4
  236.8 1.7 copy-start.8
  247.2 42.1 %all-to-all-start.1 = ((bf16[16,2,24576]{2,1,0:T(2,128)(2,1)}), bf16[16,2,24576]{2,1,0:T(2,128)(2,1)S(1)}, u32[]{:S(2)}, u32[]{:S(2)}) async-start(bf16[16,2,24576]{2,1,0:T(2,128)(2,1)} %copy.36), calls=%async_computation.2 | async-start | bytes 3145728 | tf_op jit(solution)/shard_map/all_to_all | solution.py:170
  299.6 5.5 %copy-start.1 = (bf16[1536,768]{1,0:T(8,128)(2,1)S(1)}, bf16[1536,768]{1,0:T(8,128)(2,1)}, u32[]{:S(2)}) copy-start(bf16[1536,768]{1,0:T(8,128)(2,1)} %param.12) | copy-start | bytes 7077892
Sparse Core Ops, SparseCore 0:
  12.8 80.5 all-gather.1
  222.5 77.0 reduce-scatter.1
where the time goes:
time: 315 us; the launch traced here: 312 us
  waiting for transfers between devices  115 us (37%)
  matrix products  100 us (32%)
  local copies, waits for them, and re-layouts  41.9 us (13%)
  other arithmetic  22.1 us (7%)
  between operations  14.9 us (5%)
  starting transfers between devices  12.2 us (4%)
  loops' own time  5.49 us (2%)
    all_gather x1, waiting for transfers between devices, shards(): normed_all = lax.all_gather(normed_own, 'tp', axis=0, tiled=True)  75.6 us
    sub x8, matrix products, one_block(): weights = jnp.where(allowed, jnp.exp(masked - row_max), 0.0)  53.6 us
    all_to_all x1, waiting for transfers between devices, shards(): lax.all_to_all(send_pages, 'req', split_axis=0, concat_axis=0, tiled=True)  34.8 us
    dot_general x8, matrix products, one_block(): jnp.einsum('hgqk,khd->qhgd', weights.astype(jnp.bfloat16), value_vectors,...  28.8 us
    dot_general x1, matrix products, shards(): jnp.dot(attended, w_out, preferred_element_type=jnp.float32)  7.84 us
    dot_general x1, matrix products, shards(): projected = jnp.dot(normed_all, w_qkv, preferred_element_type=jnp.float32)  7.39 us
    dynamic_update_slice x16, local copies, waits for them, and re-layouts, attend(): outputs = lax.map(one_block, (grouped, segment_blocks, numbers))  6.91 us
    another operation x3, local copies, waits for them, and re-layouts, shards(): jnp.stack([key_pages, value_pages], axis=2)  6.5 us
  transfers between devices with their start and end apart: 4, of which 3 were waited for; matrix products, arithmetic and copies ran while one was open for 9% of the time, Pallas kernels for 0%

commit v1 on v0

v1 whole, which is shorter than its diff:
```python
import jax
import jax.numpy as jnp
from jax import lax
from jax.experimental import pallas as pl
from jax.experimental.pallas import tpu as pltpu
from jax.sharding import PartitionSpec as P

HEAD = 96
HEADS_Q = 8
HEADS_KV = 4
PAGE = 64
REQS = 8


rotary_base = 100000.0
norm_eps = 1e-05
masked_score = -1e30


def rotary_tables(positions, width):
    half_width = width // 2
    exponent = jnp.arange(half_width, dtype=jnp.float32) * (2.0 / width)
    inverse = jnp.power(jnp.float32(rotary_base), -exponent)
    angles = positions.astype(jnp.float32)[:, None] * inverse[None, :]
    return (jnp.cos(angles), jnp.sin(angles))


def rotate(vectors, cosine, sine_table):
    half_width = vectors.shape[-1] // 2
    front_half = vectors[..., :half_width]
    second = vectors[..., half_width:]
    cosine = cosine[:, None, :]
    sine_table = sine_table[:, None, :]
    return jnp.concatenate(
        [front_half * cosine - second * sine_table, second * cosine + front_half * sine_table],
        axis=-1,
    )


def normalize(token_rows, gain_vector):
    values = token_rows.astype(jnp.float32)
    inverse_root = lax.rsqrt(jnp.mean(values * values, axis=-1, keepdims=True) + norm_eps)
    return (values * inverse_root * gain_vector.astype(jnp.float32)).astype(jnp.bfloat16)


Q_BLOCK = 256
K_BLOCK = 256
PIECES = 3


def weights_kernel(wq_ref, wo_ref, oq_ref, oo_ref, send_sem, recv_sem):
    req = lax.axis_index("req")
    tp = lax.axis_index("tp")
    member = lax.rem(req, 4)
    base = req - member
    core_member = member + 1 - 2 * lax.rem(member, 2)
    row_member = member + 2 - 4 * (member // 2)
    across = {"tp": 1 - tp}
    core_peer = {"req": base + core_member}
    row_peer = {"req": base + row_member}
    barrier = pltpu.get_barrier_semaphore()
    for peer in (across, core_peer, row_peer):
        pl.semaphore_signal(barrier, inc=1, device_id=peer, device_id_type=pl.DeviceIdType.MESH)
    pl.semaphore_wait(barrier, 3)

    q_rows = wq_ref.shape[0] // 4 // PIECES
    o_rows = wo_ref.shape[0] // 4

    def views(ref_q, ref_o, owner, piece):
        if piece < PIECES:
            return ref_q.at[pl.ds((owner * PIECES + piece) * q_rows, q_rows)]
        return ref_o.at[pl.ds(owner * o_rows, o_rows)]

    def copy(source, owner, piece, channel, peer):
        src = views(*source, owner, piece)
        dst = views(oq_ref, oo_ref, owner, piece)
        return pltpu.make_async_remote_copy(
            src_ref=src,
            dst_ref=dst,
            send_sem=send_sem.at[piece, channel],
            recv_sem=recv_sem.at[piece, channel],
            device_id=peer,
            device_id_type=pl.DeviceIdType.MESH,
        )

    here = (oq_ref, oo_ref)
    pieces = range(PIECES + 1)
    first = [copy((wq_ref, wo_ref), member, p, 0, across) for p in pieces]
    core_first = [copy(here, member, p, 1, core_peer) for p in pieces]
    row_first = [copy(here, member, p, 2, row_peer) for p in pieces]
    core_second = [copy(here, row_member, p, 3, core_peer) for p in pieces]
    for c in first:
        c.start()
    for p in pieces:
        first[p].wait_recv()
        row_first[p].start()
        core_first[p].start()
        if p >= 1:
            row_first[p - 1].wait_recv()
            core_second[p - 1].start()
    row_first[PIECES].wait_recv()
    core_second[PIECES].start()
    for p in pieces:
        first[p].wait_send()
        row_first[p].wait_send()
        core_first[p].wait()
        core_second[p].wait()


def other_weights(w_qkv, w_out):
    return pl.pallas_call(
        weights_kernel,
        out_shape=(
            jax.ShapeDtypeStruct(w_qkv.shape, w_qkv.dtype),
            jax.ShapeDtypeStruct(w_out.shape, w_out.dtype),
        ),
        in_specs=[pl.BlockSpec(memory_space=pl.ANY)] * 2,
        out_specs=[pl.BlockSpec(memory_space=pl.ANY)] * 2,
        scratch_shapes=[
            pltpu.SemaphoreType.DMA((PIECES + 1, 4)),
            pltpu.SemaphoreType.DMA((PIECES + 1, 4)),
        ],
        compiler_params=pltpu.CompilerParams(collective_id=0, has_side_effects=True),
        name="weights",
    )(w_qkv, w_out)


def attention_kernel(
    info_ref, blocks_ref, q_ref, kv_ref, starts_ref, wo_own_ref, wo_other_ref, hidden_ref, out_ref, mixed_ref
):
    block = pl.program_id(0)
    row_offset = info_ref[0]
    prefix = info_ref[1]
    key_offset = info_ref[2]
    prefix_end = blocks_ref[0, block]
    low = blocks_ref[1, block]
    high = blocks_ref[2, block]
    factor = HEAD ** (-0.5) * 1.4426950408889634
    local = lax.broadcasted_iota(jnp.int32, (Q_BLOCK, 1), 0) + row_offset + block * Q_BLOCK
    places = jnp.concatenate([local, local], axis=0)
    starts = starts_ref[...]
    starts = jnp.concatenate([starts, starts], axis=0)
    for head in range(HEADS_KV):
        key_row = (head // 2) * 4 + head % 2
        queries = q_ref[2 * head : 2 * head + 2].reshape(2 * Q_BLOCK, HEAD)

        def step(number, carry):
            row_max, totals, mixed = carry
            begin = pl.multiple_of(number * K_BLOCK + key_offset, K_BLOCK)
            keys = kv_ref[key_row, pl.ds(begin, K_BLOCK), :]
            values = kv_ref[key_row + 2, pl.ds(begin, K_BLOCK), :]
            scores = lax.dot_general(
                queries, keys, (((1,), (1,)), ((), ())), preferred_element_type=jnp.float32
            ) * factor
            key_places = lax.broadcasted_iota(jnp.int32, (1, K_BLOCK), 1) + number * K_BLOCK
            allowed = (key_places <= places) & ((key_places >= starts) | (key_places < prefix))
            scores = jnp.where(allowed, scores, masked_score)
            new_max = jnp.maximum(row_max, jnp.max(scores, axis=1, keepdims=True))
            weights = jnp.exp2(scores - new_max)
            scale = jnp.exp2(row_max - new_max)
            totals = totals * scale + jnp.sum(weights, axis=1, keepdims=True)
            mixed = mixed * scale + jnp.dot(
                weights.astype(jnp.bfloat16), values, preferred_element_type=jnp.float32
            )
            return new_max, totals, mixed

        carry = (
            jnp.full((2 * Q_BLOCK, 1), -1e20, jnp.float32),
            jnp.zeros((2 * Q_BLOCK, 1), jnp.float32),
            jnp.zeros((2 * Q_BLOCK, HEAD), jnp.float32),
        )
        carry = lax.fori_loop(0, prefix_end, step, carry)
        _, totals, mixed = lax.fori_loop(low, high, step, carry)
        result = (mixed / totals).astype(jnp.bfloat16)
        mixed_ref[:, 2 * head * HEAD : (2 * head + 1) * HEAD] = result[:Q_BLOCK]
        mixed_ref[:, (2 * head + 1) * HEAD : (2 * head + 2) * HEAD] = result[Q_BLOCK:]
    half = HEADS_Q * HEAD // 2
    product = jnp.dot(mixed_ref[:, :half], wo_own_ref[...], preferred_element_type=jnp.float32)
    product += jnp.dot(mixed_ref[:, half:], wo_other_ref[...], preferred_element_type=jnp.float32)
    out_ref[...] = (hidden_ref[...].astype(jnp.float32) + product).astype(jnp.bfloat16)


def attention(info, blocks, queries, keys_values, starts, wo_own, wo_other, hidden):
    tokens, width = hidden.shape
    whole = lambda shape: pl.BlockSpec(shape, lambda i, *_: (0,) * len(shape))
    return pl.pallas_call(
        attention_kernel,
        grid_spec=pltpu.PrefetchScalarGridSpec(
            num_scalar_prefetch=2,
            grid=(tokens // Q_BLOCK,),
            in_specs=[
                pl.BlockSpec((HEADS_Q, Q_BLOCK, HEAD), lambda i, *_: (0, i, 0)),
                whole(keys_values.shape),
                pl.BlockSpec((Q_BLOCK, 1), lambda i, *_: (i, 0)),
                whole(wo_own.shape),
                whole(wo_other.shape),
                pl.BlockSpec((Q_BLOCK, width), lambda i, *_: (i, 0)),
            ],
            out_specs=pl.BlockSpec((Q_BLOCK, width), lambda i, *_: (i, 0)),
            scratch_shapes=[pltpu.VMEM((Q_BLOCK, HEADS_Q * HEAD), jnp.bfloat16)],
        ),
        out_shape=jax.ShapeDtypeStruct(hidden.shape, hidden.dtype),
        compiler_params=pltpu.CompilerParams(vmem_limit_bytes=48 * 1024 * 1024),
        cost_estimate=pl.CostEstimate(
            flops=20_000_000_000, bytes_accessed=16_000_000, transcendentals=8_000_000
        ),
        name="attention",
    )(info, blocks, queries, keys_values, starts, wo_own, wo_other, hidden)


def heads_of(projected, cosine, sine_table):
    tokens = projected.shape[0]
    local_query, local_kv = HEADS_Q // 2, HEADS_KV // 2
    turned = rotate(
        projected[:, : (local_query + local_kv) * HEAD].reshape(tokens, -1, HEAD), cosine, sine_table
    ).astype(jnp.bfloat16)
    values = projected[:, (local_query + local_kv) * HEAD :].reshape(tokens, local_kv, HEAD)
    return (
        turned[:, :local_query],
        jnp.concatenate([turned[:, local_query:], values.astype(jnp.bfloat16)], axis=1).reshape(tokens, -1),
    )


def shards(hidden_in, segment_ids, page_owner, norm_gain, w_qkv, w_out):
    req_count = lax.axis_size("req")
    tp = lax.axis_index("tp")
    group_len = segment_ids.shape[0]
    tokens = hidden_in.shape[0]
    local_kv = HEADS_KV // 2
    row_offset = tp * tokens
    numbers = jnp.arange(REQS + 2, dtype=jnp.int32)
    firsts = jnp.sum((segment_ids[None, :] < numbers[:, None]).astype(jnp.int32), axis=1)
    prefix = firsts[1]
    own_segments = lax.dynamic_slice(segment_ids, (row_offset,), (tokens,))
    starts = jnp.sum(
        jnp.where(own_segments[:, None] == numbers[None, :], firsts[None, :], 0), axis=1
    )
    places = row_offset + jnp.arange(tokens, dtype=jnp.int32)
    positions = places - starts + jnp.where(own_segments > 0, prefix, 0)
    cosine, sine_table = rotary_tables(positions, HEAD)
    wq_other, wo_other = other_weights(w_qkv, w_out)
    normed = normalize(hidden_in, norm_gain)
    queries_own, kv_own = heads_of(
        jnp.dot(normed, w_qkv, preferred_element_type=jnp.float32), cosine, sine_table
    )
    queries_other, kv_other = heads_of(
        jnp.dot(normed, wq_other, preferred_element_type=jnp.float32), cosine, sine_table
    )
    peer_own = lax.ppermute(kv_other, "tp", [(0, 1), (1, 0)])
    peer_other = lax.ppermute(kv_own, "tp", [(0, 1)])
    cached = jnp.concatenate([peer_own, kv_own], axis=0)
    keys_values = jnp.concatenate(
        [cached, jnp.concatenate([peer_other, kv_other], axis=0)], axis=1
    )
    keys_values = keys_values.reshape(group_len, 2 * HEADS_KV, HEAD).transpose(1, 0, 2)
    queries = jnp.concatenate([queries_own, queries_other], axis=1).transpose(1, 0, 2)

    block_count = tokens // Q_BLOCK
    block_numbers = jnp.arange(block_count, dtype=jnp.int32)
    high = (row_offset + (block_numbers + 1) * Q_BLOCK) // K_BLOCK
    prefix_end = jnp.minimum((prefix + K_BLOCK - 1) // K_BLOCK, high)
    low = jnp.maximum(starts[::Q_BLOCK] // K_BLOCK, prefix_end)
    blocks = jnp.stack([prefix_end, low, high])
    info = jnp.stack([row_offset, prefix, (1 - tp) * tokens])

    page_count = group_len // PAGE
    lane_count = -(-page_count // req_count)
    page_numbers = jnp.arange(page_count, dtype=jnp.int32)
    live_pages = segment_ids[::PAGE] != REQS + 1
    half_pages = page_count // 2
    swap = lambda x: jnp.where(tp == 0, jnp.roll(x, half_pages), x)
    local_numbers, local_owner, local_live = swap(page_numbers), swap(page_owner), swap(live_pages)
    page_data = (
        cached.reshape(page_count, PAGE, 2, local_kv, HEAD)
        .transpose(0, 3, 2, 1, 4)
        .reshape(page_count, local_kv * 2 * PAGE * HEAD)
    )
    same_owner = (
        (local_owner[:, None] == local_owner[None, :])
        & local_live[None, :]
        & (local_numbers[None, :] < local_numbers[:, None])
    )
    page_rank = jnp.sum(same_owner.astype(jnp.int32), axis=1)
    owner_ids = jnp.arange(req_count, dtype=jnp.int32)
    lane_ids = jnp.arange(lane_count, dtype=jnp.int32)
    selection = (
        (local_owner[None, None, :] == owner_ids[:, None, None])
        & (page_rank[None, None, :] == lane_ids[None, :, None])
        & local_live[None, None, :]
    )
    send_pages = jnp.einsum(
        "olp,pc->olc", selection.astype(jnp.bfloat16), page_data, preferred_element_type=jnp.float32
    ).astype(jnp.bfloat16)
    send_ids = jnp.sum(jnp.where(selection, local_numbers[None, None, :] + 1, 0), axis=2) - 1
    received_ids = lax.all_to_all(send_ids, "req", split_axis=0, concat_axis=0, tiled=True)
    received = lax.all_to_all(send_pages, "req", split_axis=0, concat_axis=0, tiled=True)
    hidden_out = attention(info, blocks, queries, keys_values, starts[:, None], w_out, wo_other, hidden_in)
    placing = (
        received_ids.reshape(req_count * lane_count)[None, :] == page_numbers[:, None]
    ).astype(jnp.bfloat16)
    cache_rows = jnp.dot(
        placing,
        received.reshape(req_count * lane_count, local_kv * 2 * PAGE * HEAD),
        preferred_element_type=jnp.float32,
    ).astype(jnp.bfloat16)
    return (hidden_out, cache_rows.reshape(page_count, local_kv, 2, PAGE * HEAD))


def solution(mesh):
    placed = (P(("req", "tp"), None), P("req"), P("req"), P(), P(None, "tp"), P("tp", None))
    return jax.shard_map(
        shards,
        mesh=mesh,
        in_specs=placed,
        out_specs=(P(("req", "tp"), None), P("req", "tp", None, None)),
        check_vma=False,
    )
```

time: 315 us -> 211 us (0.67)
  waiting for transfers between devices: 115 us -> 9.6 us
  Pallas kernels: 0 us -> 89.6 us
  matrix products: 100 us -> 11.2 us
  local copies, waits for them, and re-layouts: 41.9 us -> 56.7 us
  between operations: 14.9 us -> 1.64 us
  loops' own time: 5.49 us -> 0 us
    pallas_call x0 -> x2, Pallas kernels: none -> 89.6 us  [the longest x1 59.1 us: attention(): pl.pallas_call(attention_kernel, grid_spec=pltpu.PrefetchScalarGridSpec(n...]
    all_gather x1 -> x0, waiting for transfers between devices: 75.6 us -> none  [shards(): normed_all = lax.all_gather(normed_own, 'tp', axis=0, tiled=True)]
    sub x8 -> x0, matrix products: 53.6 us -> none  [one_block(): weights = jnp.where(allowed, jnp.exp(masked - row_max), 0.0)]
    all_to_all x1, waiting for transfers between devices: 34.8 us -> 0.01 us  [shards(): lax.all_to_all(send_pages, 'req', split_axis=0, concat_axis=0, tiled=True)]
    dot_general x10 -> x2, matrix products: 44.1 us -> 10 us  [the longest x1 5.53 us: shards(): jnp.dot(normed, wq_other, preferred_element_type=jnp.float32)]
    reshape x2 -> x3, local copies, waits for them, and re-layouts: 2.42 us -> 16.8 us  [the longest x1 6.26 us: shards(): keys_values.reshape(group_len, 2 * HEADS_KV, HEAD).transpose(1, 0, 2)]
    ppermute x0 -> x2, waiting for transfers between devices: none -> 9.6 us  [the longest x1 9.59 us: shards(): peer_own = lax.ppermute(kv_other, 'tp', [(0, 1), (1, 0)])]
    unnamed x27 -> x26, local copies, waits for them, and re-layouts: 5.72 us -> 14.9 us
  transfers between devices with their start and end apart: 4 -> 4, of which waited for: 3 -> 1; matrix products, arithmetic and copies ran while one was open for 9% -> 17% of each run, Pallas kernels for 0% -> 29%
where the time goes in v1:
time: 211 us; the launch traced here: 207 us
  Pallas kernels  89.6 us (42%)
  local copies, waits for them, and re-layouts  56.7 us (27%)
  other arithmetic  23.2 us (11%)
  starting transfers between devices  15.3 us (7%)
  matrix products  11.2 us (5%)
  waiting for transfers between devices  9.6 us (5%)
    pallas_call x1, Pallas kernels, attention(): pl.pallas_call(attention_kernel, grid_spec=pltpu.PrefetchScalarGridSpec(n...  59.1 us
    pallas_call x1, Pallas kernels, other_weights(): pl.pallas_call(weights_kernel, out_shape=(jax.ShapeDtypeStruct(w_qkv.shap...  30.5 us
    unnamed x26, local copies, waits for them, and re-layouts  14.9 us
    ppermute x1, waiting for transfers between devices, shards(): peer_own = lax.ppermute(kv_other, 'tp', [(0, 1), (1, 0)])  9.59 us
    all_to_all x1, starting transfers between devices, shards(): lax.all_to_all(send_pages, 'req', split_axis=0, concat_axis=0, tiled=True)  6.27 us
    reshape x1, local copies, waits for them, and re-layouts, shards(): keys_values.reshape(group_len, 2 * HEADS_KV, HEAD).transpose(1, 0, 2)  6.26 us
    reshape x1, local copies, waits for them, and re-layouts, shards(): cached.reshape(page_count, PAGE, 2, local_kv, HEAD).transpose(0, 3, 2, 1, 4)  6.26 us
    all_to_all x1, starting transfers between devices, shards(): lax.all_to_all(send_ids, 'req', split_axis=0, concat_axis=0, tiled=True)  6.23 us
  transfers between devices with their start and end apart: 4, of which 1 were waited for; matrix products, arithmetic and copies ran while one was open for 17% of the time, Pallas kernels for 29%

profile of v1, /device:TPU:14, one launch (start us, length us, event | category | flops | bytes accessed | tf_op | source)
XLA Modules:
  0.0 207.3 jit_solution(11978634325578353025)
XLA Ops:
  0.7 2.7 %fusion = f32[1024]{0:T(1024)S(1)} fusion(bf16[1024,1536]{1,0:T(8,128)(2,1)} %hidden_ref.1), kind=kLoop, calls=%fused_computation.4 | loop fusion | flops 4717568 | bytes 3149824 | tf_op jit(solution)/shard_map/reduce_sum | solution.py:42
  3.5 4.5 %fusion.9 = f32[1024,768]{0,1:T(8,128)S(1)} fusion(bf16[1536,768]{1,0:T(8,128)(2,1)} %wq_ref.1, bf16[1024,1536]{1,0:T(8,128)(2,1)S(1)} %copy-done.4, f32[1536]{0:T(1024)S(1)} %convert_element_type.38, f32[1024]{0:T(1024)S(1)} %add_rsqrt_fusion), kind=kOutput, calls=%fused_computation.25 | convolution fusion | flops 2422210560 | bytes 8660992 | tf_op jit(solution)/shard_map/dot_general | solution.py:244
  9.8 30.5 %weights.1 = (bf16[1536,768]{1,0:T(8,128)(2,1)}, bf16[384,1536]{1,0:T(8,128)(2,1)}) custom-call(bf16[1536,768]{1,0:T(8,128)(2,1)} %wq_ref.1, bf16[384,1536]{1,0:T(8,128)(2,1)} %wo_own_ref.1), custom_call_target="tpu_custom_call" | custom-call | tf_op jit(solution)/shard_map/weights/pallas_call | solution.py:111
  40.3 5.5 %fusion.7 = f32[1024,768]{0,1:T(8,128)S(1)} fusion(bf16[1536,768]{1,0:T(8,128)(2,1)} %get-tuple-element.4, bf16[1024,1536]{1,0:T(8,128)(2,1)} %hidden_ref.1, f32[1536]{0:T(1024)S(1)} %convert_element_type.38, f32[1024]{0:T(1024)S(1)} %add_rsqrt_fusion), kind=kOutput, calls=%fused_computation.24 | convolution fusion | flops 2422210560 | bytes 8660992 | tf_op jit(solution)/shard_map/dot_general | solution.py:247
  46.0 1.6 slice.95
  48.5 1.6 fusion.15
  51.1 2.0 copy.51
  53.2 3.2 %copy.52 = f32[1024,6,48]{2,0,1:T(8,128)} copy(f32[1024,6,48]{0,2,1:T(8,128)} %get-tuple-element.17) | data formatting | bytes 2359296
  56.4 3.4 %fusion.16 = (f32[1024,6,48]{0,2,1:T(8,128)}, f32[1024,6,48]{0,2,1:T(8,128)}) fusion(f32[1024,6,96]{0,2,1:T(8,128)} %bitcast.27), kind=kLoop, calls=%fused_computation.70 | loop fusion | bytes 4718592 | tf_op jit(solution)/shard_map/slice | solution.py:30
  60.8 3.2 %copy.53 = f32[1024,6,48]{2,0,1:T(8,128)} copy(f32[1024,6,48]{0,2,1:T(8,128)} %get-tuple-element.18) | data formatting | bytes 2359296
  64.0 3.2 %copy.54 = f32[1024,6,48]{2,0,1:T(8,128)} copy(f32[1024,6,48]{0,2,1:T(8,128)} %get-tuple-element.19) | data formatting | bytes 2359296
  67.9 1.9 multiply_cosine_fusion
  69.8 4.8 %add_convert_fusion.1 = (bf16[1024,6,48]{2,0,1:T(8,128)(2,1)S(1)}, bf16[1024,6,48]{2,0,1:T(8,128)(2,1)S(1)}, bf16[1024,6,48]{2,0,1:T(8,128)(2,1)S(1)}, bf16[1024,6,48]{2,0,1:T(8,128)(2,1)S(1)}) fusion(f32[1024,6,48]{2,0,1:T(8,128)S(1)} %copy.51, f32[1024,6,48]{2,0,1:T(8,128)} %copy.52, f32[1024,48]{1,0:T(8,128)S(1)} %get-tuple-element.23, ...), kind=kLoop, calls=%fused_computation.10 | loop fusion | flops 4718592 | bytes 7471104 | tf_op jit(solution)/shard_map/convert.5
  74.6 4.1 %fusion.5 = (bf16[1024,4,96]{2,0,1:T(8,128)(2,1)S(1)}, bf16[1024,4,96]{2,0,1:T(8,128)(2,1)}, bf16[1024,4,96]{2,0,1:T(8,128)(2,1)}, bf16[1024,4,96]{2,0,1:T(8,128)(2,1)S(1)}) fusion(bf16[1024,6,48]{2,0,1:T(8,128)(2,1)S(1)} %get-tuple-element.8, bf16[1024,6,48]{2,0,1:T(8,128)(2,1)S(1)} %get-tuple-element.9, bf16[1024,2,96]{2,0,1:T(8,128)(2,1)S(1)} %copy-done.5, ...), kind=kLoop, calls=%fused_computation.21 | loop fusion | flops 7864320 | bytes 6291456 | tf_op jit(solution)/shard_map/concatenate | solution.py:220
  78.7 1.3 copy.42
  80.0 1.5 collective-permute-start
  83.0 6.2 %all-to-all-start = ((s32[16,1,2]{2,1,0:T(1,128)}), s32[16,1,2]{2,1,0:T(1,128)S(1)}, u32[]{:S(2)}, u32[]{:S(2)}) async-start(s32[16,1,2]{2,1,0:T(1,128)} %copy.47), calls=%async_computation | async-start | bytes 16384 | tf_op jit(solution)/shard_map/all_to_all | solution.py:295
  89.8 1.3 collective-permute-start.1
  91.1 9.6 %collective-permute-done = bf16[1024,384]{0,1:T(8,128)(2,1)} collective-permute-done((bf16[1024,384]{0,1:T(8,128)(2,1)}, bf16[1024,384]{0,1:T(8,128)(2,1)}, u32[]{:S(2)}, u32[]{:S(2)}) %collective-permute-start) | collective-permute-done | bytes 786464 | tf_op jit(solution)/shard_map/ppermute | solution.py:249
  101.9 1.8 copy.48
  103.7 6.3 %reshape.284 = bf16[32,64,2,2,96]{4,3,2,1,0:T(2,128)(2,1)S(1)} reshape(bf16[2048,384]{1,0:T(8,128)(2,1)} %copy.48) | data formatting | bytes 3145728 | tf_op jit(solution)/shard_map/reshape | solution.py:274
  110.0 1.9 copy.49
  111.9 4.2 %reshape.288 = bf16[32,24576,1]{1,0,2:T(8,128)(2,1)S(1)} reshape(bf16[32,2,2,64,96]{4,3,2,1,0:T(8,128)(2,1)} %copy.49) | data formatting | bytes 3145728 | tf_op jit(solution)/shard_map/reshape | solution.py:276
  116.7 2.8 %copy.50 = bf16[16,2,24576]{2,1,0:T(2,128)(2,1)} copy(bf16[16,2,24576]{2,0,1:T(8,128)(2,1)S(1)} %convolution_convert_fusion.1) | data formatting | bytes 3145728 | tf_op jit(solution)/shard_map/convert_element_type | solution.py:293
  119.5 6.3 %all-to-all-start.1 = ((bf16[16,2,24576]{2,1,0:T(2,128)(2,1)}), bf16[16,2,24576]{2,1,0:T(2,128)(2,1)}, u32[]{:S(2)}, u32[]{:S(2)}) async-start(bf16[16,2,24576]{2,1,0:T(2,128)(2,1)} %copy.50), calls=%async_computation.1 | async-start | bytes 3145728 | tf_op jit(solution)/shard_map/all_to_all | solution.py:296
  128.4 2.0 maximum_bitcast_fusion.q_ref
  131.6 3.6 %maximum_maximum_fusion = bf16[2048,768]{0,1:T(8,128)(2,1)} fusion(bf16[1024,384]{0,1:T(8,128)(2,1)} %bitcast.8, bf16[1024,384]{0,1:T(8,128)(2,1)} %collective-permute-done.1, bf16[1024,384]{0,1:T(8,128)(2,1)S(1)} %bitcast.32, bf16[1024,384]{0,1:T(8,128)(2,1)} %collective-permute-done), kind=kLoop, calls=%fused_computation.7 | loop fusion | flops 12582912 | bytes 6291456 | tf_op jit(solution)/shard_map/concatenate | solution.py:252
  135.2 6.3 %copy.45 = bf16[2048,8,96]{2,0,1:T(8,128)(2,1)} copy(bf16[2048,8,96]{0,2,1:T(8,128)(2,1)} %bitcast.26) | data formatting | bytes 6291456 | tf_op jit(solution)/shard_map/reshape | solution.py:255
  142.5 1.3 copy-done.2
  143.8 59.1 %attention.1 = bf16[1024,1536]{1,0:T(8,128)(2,1)} custom-call(s32[3]{0:T(128)S(1)} %pad_add_fusion.1.info_ref, s32[3,4]{1,0:T(4,128)S(1)} %pad_add_fusion.blocks_ref, bf16[8,1024,96]{2,1,0:T(8,128)(2,1)S(1)} %maximum_bitcast_fusion.q_ref, bf16[8,2048,96]{2,1,0:T(8,128)(2,1)} %bitcast.33, s32[1024,1]{1,0:T(8,128)S(1)} %copy-done.1, ...), custom_call_target="tpu_custom_call" | custom-call | flops 20000000000 | bytes 16000000 | tf_op jit(solution)/shard_map/attention/pallas_call | solution.py:186
  202.9 1.8 reshape.286
  205.2 2.1 reshape.287
  (66 shorter events, 14.3 us)
Async XLA Ops:
  0.6 2.9 %copy-start.4 = (bf16[1024,1536]{1,0:T(8,128)(2,1)S(1)}, bf16[1024,1536]{1,0:T(8,128)(2,1)}, u32[]{:S(2)}) copy-start(bf16[1024,1536]{1,0:T(8,128)(2,1)} %hidden_ref.1) | copy-start | bytes 9437188
  0.6 2.8 %copy-start.10 = (bf16[1536]{0:T(1024)(128)(2,1)S(1)}, bf16[1536]{0:T(1024)(128)(2,1)}, u32[]{:S(2)}) copy-start(bf16[1536]{0:T(1024)(128)(2,1)} %param.9) | copy-start | bytes 9220
  8.0 1.8 copy-start.3
  45.9 1.6 copy-start.8
  45.9 2.5 %slice-start = ((f32[1024,768]{0,1:T(8,128)}), f32[1024,576]{0,1:T(8,128)S(1)}, s32[]{:S(2)}) async-start(f32[1024,768]{0,1:T(8,128)} %copy-done.3), calls=%async_computation.2 | async-start | bytes 4718592 | tf_op jit(solution)/shard_map/slice | solution.py:215
  48.5 1.6 copy-start.7
  69.8 4.8 %copy-start.5 = (bf16[1024,2,96]{2,0,1:T(8,128)(2,1)S(1)}, bf16[1024,2,96]{2,0,1:T(8,128)(2,1)}, u32[]{:S(2)}) copy-start(bf16[1024,2,96]{2,0,1:T(8,128)(2,1)} %copy.43) | copy-start | bytes 1179652
  69.8 4.8 %copy-start.6 = (bf16[1024,2,96]{2,0,1:T(8,128)(2,1)S(1)}, bf16[1024,2,96]{2,0,1:T(8,128)(2,1)}, u32[]{:S(2)}) copy-start(bf16[1024,2,96]{2,0,1:T(8,128)(2,1)} %copy.41) | copy-start | bytes 1179652
  74.6 7.2 %copy-start.9 = (s32[32]{0:T(128)S(1)}, s32[32]{0:T(128)}, u32[]{:S(2)}) copy-start(s32[32]{0:T(128)} %param.8) | copy-start | bytes 388
  80.0 20.7 %collective-permute-start = (bf16[1024,384]{0,1:T(8,128)(2,1)}, bf16[1024,384]{0,1:T(8,128)(2,1)}, u32[]{:S(2)}, u32[]{:S(2)}) collective-permute-start(bf16[1024,384]{0,1:T(8,128)(2,1)} %bitcast.8), channel_id=1, source_target_pairs={{0,1},{1,0},{2,3},{3,2},{4,5},{5,4},{6,7},{7,6},{8,9},{9,8},{10,11... | collective-permute-start | bytes 2359304 | tf_op jit(solution)/shard_map/ppermute | solution.py:249
  83.0 36.4 %all-to-all-start = ((s32[16,1,2]{2,1,0:T(1,128)}), s32[16,1,2]{2,1,0:T(1,128)S(1)}, u32[]{:S(2)}, u32[]{:S(2)}) async-start(s32[16,1,2]{2,1,0:T(1,128)} %copy.47), calls=%async_computation | async-start | bytes 16384 | tf_op jit(solution)/shard_map/all_to_all | solution.py:295
  89.8 41.8 %collective-permute-start.1 = (bf16[1024,384]{0,1:T(8,128)(2,1)S(1)}, bf16[1024,384]{0,1:T(8,128)(2,1)}, u32[]{:S(2)}, u32[]{:S(2)}) collective-permute-start(bf16[1024,384]{0,1:T(8,128)(2,1)S(1)} %bitcast.30), channel_id=1, source_target_pairs={{0,1},{2,3},{4,5},{6,7},{8,9},{10,11},{12,13},{14,15},{16,17},{18,... | collective-permute-start | bytes 2359304 | tf_op jit(solution)/shard_map/ppermute | solution.py:250
  119.5 83.5 %all-to-all-start.1 = ((bf16[16,2,24576]{2,1,0:T(2,128)(2,1)}), bf16[16,2,24576]{2,1,0:T(2,128)(2,1)}, u32[]{:S(2)}, u32[]{:S(2)}) async-start(bf16[16,2,24576]{2,1,0:T(2,128)(2,1)} %copy.50), calls=%async_computation.1 | async-start | bytes 3145728 | tf_op jit(solution)/shard_map/all_to_all | solution.py:296
  135.2 6.3 %copy-start = (bf16[384,1536]{1,0:T(8,128)(2,1)S(1)}, bf16[384,1536]{1,0:T(8,128)(2,1)}, u32[]{:S(2)}) copy-start(bf16[384,1536]{1,0:T(8,128)(2,1)} %wo_own_ref.1) | copy-start | bytes 3538948
  141.5 1.0 copy-start.1
  142.5 1.3 copy-start.2
